TPU v7x, 32 devices: a whole 2x2x4 slice. The times are simulated.
32 devices in a mesh: group: 2 (over x), expert: 16 (over z, y, core).
Axes of the slice: x: 2, y: 2, z: 4, core: 2. Of those that a mesh axis runs over, the one named last changes fastest.
Arguments:
- tokens: bfloat16 [1536, 3584], P(('group', 'expert')), parts along dimension 0, may hold values from -6 to 6
- tangent: bfloat16 [1536, 3584], P(('group', 'expert')), parts along dimension 0, may hold values from -6 to 6
- routes: int32 [1536, 8], P(('group', 'expert')), parts along dimension 0, may hold values from 0 to 15, all different within a row; in each aligned block of 48 rows (0 to 47, 48 to 95, ...) at most 32 rows name the same one
- gates: float32 [1536, 8], P(('group', 'expert')), parts along dimension 0, may hold values from 0.1 to 1
- probes: float32 [1536, 16], P(('group', 'expert')), parts along dimension 0, may hold values from -0.21875 to 0.21875
- w_gate: bfloat16 [16, 3584, 1024], P('expert'), may hold values from -0.09375 to 0.09375
- w_up: bfloat16 [16, 3584, 1024], P('expert'), may hold values from -0.09375 to 0.09375
- w_down: bfloat16 [16, 1024, 3584], P('expert'), may hold values from -0.1875 to 0.1875
Outputs:
- curvature_rows: bfloat16 [1536, 3584], P(('group', 'expert')), parts along dimension 0
- sketch: float32 [32, 3584], P('group', 'expert'), parts along dimension 0
There are 2 independent parts, one for each index of `group`. A program takes and returns all parts, laid end to end along the dimension named above; an argument that names none is the same for every part. Nothing has to cross between parts.
Inputs may be any that keep to these rules, and one draw needn't show every extreme that they name: `routes`: within one row the 8 experts differ. In each aligned block of 48 rows (the rows of one device) no expert is named by more than 32 rows, a bound that some block reaches.
All inputs are finite; a program needn't handle non-finite values.
Results may differ from a plain program's by a relative error of at most 0.0075.
Values may be sent and summed in bfloat16 or wider, within the bound.
No kernel may reach another device: no remote copies, remote signals or barrier semaphores. Data moves between devices by JAX's collectives and lax.ppermute only.
A program may use at most 128 MiB of HBM per device.

v0:
```python
import jax
import jax.numpy as jnp
from jax import lax
from jax.sharding import PartitionSpec as P


def dsilu(value):
    sig = jax.nn.sigmoid(value)
    return sig * (1.0 + value * (1.0 - sig))


def body(tokens, tangent, routes, gates, probes, w_gate, w_up, w_down):
    rows, width = tokens.shape
    topk = routes.shape[1]
    count = lax.axis_size("expert")
    cap = rows * topk * 4 // (3 * count)
    flat = routes.reshape(-1)
    total = flat.shape[0]
    onehot = (flat[:, None] == jnp.arange(count, dtype=jnp.int32)[None, :]).astype(jnp.int32)
    before = jnp.cumsum(onehot, axis=0) - onehot
    slot_rank = jnp.sum(before * onehot, axis=1)
    place = flat * cap + slot_rank
    owner = jnp.arange(total, dtype=jnp.int32) // topk
    source = jnp.full((count * cap,), rows, jnp.int32).at[place].set(owner)

    def spread(values):
        padded = jnp.concatenate([values, jnp.zeros((1, width), values.dtype)], axis=0)
        return jnp.take(padded, source, axis=0).reshape(count, cap, width)

    def collect(returned):
        picked = jnp.take(returned.reshape(count * cap, width), place, axis=0)
        return picked.reshape(rows, topk, width).astype(jnp.float32)

    got_x = lax.all_to_all(spread(tokens), "expert", split_axis=0, concat_axis=0, tiled=True)
    got_t = lax.all_to_all(spread(tangent), "expert", split_axis=0, concat_axis=0, tiled=True)
    w_g = w_gate[0]
    w_u = w_up[0]
    w_d = w_down[0]
    in_rows = got_x.reshape(count * cap, width)
    in_tans = got_t.reshape(count * cap, width)
    pre_a = jnp.dot(in_rows, w_g, preferred_element_type=jnp.float32)
    pre_b = jnp.dot(in_rows, w_u, preferred_element_type=jnp.float32)
    tan_a = jnp.dot(in_tans, w_g, preferred_element_type=jnp.float32)
    tan_b = jnp.dot(in_tans, w_u, preferred_element_type=jnp.float32)
    silu_a = jax.nn.silu(pre_a)
    slope_a = dsilu(pre_a)
    hidden = (slope_a * tan_a * pre_b + silu_a * tan_b).astype(jnp.bfloat16)
    tout = jnp.dot(hidden, w_d, preferred_element_type=jnp.float32).astype(jnp.bfloat16)
    returned = lax.all_to_all(
        tout.reshape(count, cap, width), "expert", split_axis=0, concat_axis=0, tiled=True
    )
    combined = jnp.sum(gates[:, :, None] * collect(returned), axis=1).astype(jnp.bfloat16)
    got_c = lax.all_to_all(spread(combined), "expert", split_axis=0, concat_axis=0, tiled=True)
    grad_h = lax.dot_general(
        got_c.reshape(count * cap, width),
        w_d,
        (((1,), (1,)), ((), ())),
        preferred_element_type=jnp.float32,
    )
    grad_a = (grad_h * pre_b * slope_a).astype(jnp.bfloat16)
    grad_b = (grad_h * silu_a).astype(jnp.bfloat16)
    back = lax.dot_general(
        grad_a, w_g, (((1,), (1,)), ((), ())), preferred_element_type=jnp.float32
    )
    back = back + lax.dot_general(
        grad_b, w_u, (((1,), (1,)), ((), ())), preferred_element_type=jnp.float32
    )
    back = back.astype(jnp.bfloat16).reshape(count, cap, width)
    returned_q = lax.all_to_all(back, "expert", split_axis=0, concat_axis=0, tiled=True)
    curvature_rows = jnp.sum(gates[:, :, None] * collect(returned_q), axis=1).astype(jnp.bfloat16)
    term = lax.dot_general(
        probes,
        curvature_rows.astype(jnp.float32),
        (((0,), (0,)), ((), ())),
        precision=lax.Precision.HIGHEST,
        preferred_element_type=jnp.float32,
    )
    sketch = lax.psum_scatter(term, "expert", scatter_dimension=1, tiled=True)
    return (curvature_rows, sketch)


def solution(mesh):
    return jax.shard_map(
        body,
        mesh=mesh,
        in_specs=(
            P(("group", "expert"), None),
            P(("group", "expert"), None),
            P(("group", "expert"), None),
            P(("group", "expert"), None),
            P(("group", "expert"), None),
            P("expert", None, None),
            P("expert", None, None),
            P("expert", None, None),
        ),
        out_specs=(P(("group", "expert"), None), P("group", "expert")),
        check_vma=False,
    )
```

profile of v0, /device:TPU:0, one launch (start us, length us, event | category | flops | bytes accessed | tf_op | source)
XLA Modules:
  0.0 618.3 jit_solution(7613896733554713937)
XLA Ops:
  7.2 0.0 copy-start
  7.2 0.7 broadcast_multiply_fusion
  7.9 0.8 copy.17
  8.6 0.1 eq.25
  8.7 0.1 eq.29
  8.8 0.1 copy.20
  8.9 0.1 mul.68
  9.0 0.9 reduce-window.6
  9.9 0.2 slice_reduce_fusion
  10.1 0.1 fusion.32
  10.3 2.9 scatter_custom_fusion
  13.2 1.0 concatenate.9
  14.2 1.0 concatenate.10
  15.3 4.2 gather_fusion.1
  19.4 4.2 gather_fusion
  23.6 4.8 broadcast_select_fusion.1
  28.4 88.3 %all_to_all.25 = bf16[16,32,3584]{2,1,0:T(8,128)(2,1)} all-to-all(bf16[16,32,3584]{2,1,0:T(8,128)(2,1)S(1)} %bitcast.77), channel_id=1, replica_groups=mesh['group'=2,'expert'=16] {'expert'}, dimensions={0} | all-to-all | bytes 7340032 | tf_op jit(solution)/shard_map/all_to_all | solution.py:34
  116.7 5.8 all-to-all-start.1
  122.5 0.0 copy-start.1
  122.5 7.4 %fusion.14 = f32[512,1024]{1,0:T(8,128)S(1)} fusion(bf16[512,3584]{1,0:T(8,128)(2,1)} %bitcast.81, bf16[1,3584,1024]{2,1,0:T(8,128)(2,1)} %param.17), kind=kOutput, calls=%fused_computation.20 | convolution fusion | flops 3758096384 | bytes 13107200 | tf_op jit(solution)/shard_map/dot_general | solution.py:41
  130.0 0.0 copy-done.1
  130.0 0.0 copy-start.4
  130.0 8.4 %fusion.8 = f32[512,1024]{1,0:T(8,128)} fusion(bf16[512,3584]{1,0:T(8,128)(2,1)S(1)} %bitcast.82, bf16[1,3584,1024]{2,1,0:T(8,128)(2,1)} %param.18), kind=kOutput, calls=%fused_computation.14 | convolution fusion | flops 3758096384 | bytes 13107200 | tf_op jit(solution)/shard_map/dot_general | solution.py:42
  138.3 52.7 %all-to-all-done.1 = bf16[16,32,3584]{2,1,0:T(8,128)(2,1)} async-done(((bf16[16,32,3584]{2,1,0:T(8,128)(2,1)}), bf16[16,32,3584]{2,1,0:T(8,128)(2,1)}, u32[]{:S(2)}, u32[]{:S(2)}) %all-to-all-start.1) | async-done | bytes 3670048 | tf_op jit(solution)/shard_map/all_to_all | solution.py:35
  191.0 9.6 %fusion.6 = f32[512,1024]{1,0:T(8,128)} fusion(bf16[512,3584]{1,0:T(8,128)(2,1)} %bitcast.5, bf16[1,3584,1024]{2,1,0:T(8,128)(2,1)} %param.18), kind=kOutput, calls=%fused_computation.12 | convolution fusion | flops 3758096384 | bytes 13107200 | tf_op jit(solution)/shard_map/dot_general | solution.py:44
  200.6 0.0 copy-done.4
  200.6 17.7 %fusion.18 = bf16[512,3584]{1,0:T(8,128)(2,1)} fusion(bf16[1,1024,3584]{2,1,0:T(8,128)(2,1)} %param.19, f32[512,1024]{1,0:T(8,128)} %fusion.6, f32[512,1024]{1,0:T(8,128)} %fusion.8, bf16[512,3584]{1,0:T(8,128)(2,1)} %bitcast.5, bf16[1,3584,1024]{2,1,0:T(8,128)(2,1)} %param.17, f32[512,1024]{1,0:T(8,128)S(1)} %fusion.14), kind=kOutput, calls=%fused_computation.23 | convolution fusion | flops 7524843520 | bytes 28311552 | tf_op jit(solution)/shard_map/dot_general | solution.py:48
  218.4 0.0 copy-start.3
  218.4 17.7 %all-to-all-start.2 = ((bf16[16,32,3584]{2,1,0:T(8,128)(2,1)}), bf16[16,32,3584]{2,1,0:T(8,128)(2,1)}, u32[]{:S(2)}, u32[]{:S(2)}) async-start(bf16[16,32,3584]{2,1,0:T(8,128)(2,1)} %bitcast.80), calls=%async_computation.2 | async-start | bytes 7340032 | tf_op jit(solution)/shard_map/all_to_all | solution.py:49
  236.1 0.2 reduce-scatter.4.cloned.1.call-start
  236.3 0.0 copy-done.3
  236.3 0.1 copy.16
  236.4 68.2 %all-to-all-done.2 = bf16[16,32,3584]{2,1,0:T(8,128)(2,1)} async-done(((bf16[16,32,3584]{2,1,0:T(8,128)(2,1)}), bf16[16,32,3584]{2,1,0:T(8,128)(2,1)}, u32[]{:S(2)}, u32[]{:S(2)}) %all-to-all-start.2) | async-done | bytes 3670048 | tf_op jit(solution)/shard_map/all_to_all | solution.py:49
  304.6 9.4 %gather_fusion.2 = bf16[384,3584]{1,0:T(8,128)(2,1)S(1)} fusion(bf16[512,3584]{1,0:T(8,128)(2,1)} %bitcast.9, s32[1024]{0:T(1024)S(1)} %pad_clamp_fusion), kind=kCustom, calls=%fused_computation.1.clone | custom fusion | bytes 5506560 | tf_op jit(solution)/shard_map/jit(_take)/gather | solution.py:31
  314.0 2.9 fusion.22
  316.9 4.2 gather_fusion.3
  321.1 2.4 broadcast_select_fusion.2
  323.5 0.0 slice-start
  323.6 98.8 %all_to_all.26 = bf16[16,32,3584]{2,1,0:T(8,128)(2,1)S(1)} all-to-all(bf16[16,32,3584]{2,1,0:T(8,128)(2,1)S(1)} %bitcast.78), channel_id=1, replica_groups=mesh['group'=2,'expert'=16] {'expert'}, dimensions={0} | all-to-all | bytes 7340032 | tf_op jit(solution)/shard_map/all_to_all | solution.py:53
  422.4 0.0 slice-start.1
  422.4 0.0 copy-start.5
  422.4 6.4 %fusion = f32[512,1024]{1,0:T(8,128)S(1)} fusion(bf16[512,3584]{1,0:T(8,128)(2,1)S(1)} %bitcast.84, bf16[1,1024,3584]{2,1,0:T(8,128)(2,1)} %param.19), kind=kOutput, calls=%fused_computation.6 | convolution fusion | flops 3758096384 | bytes 13107200 | tf_op jit(solution)/shard_map/dot_general | solution.py:54
  428.8 0.0 copy-start.6
  428.8 1.3 copy-done.6
  430.1 0.0 slice-done
  430.1 0.0 slice-done.1
  430.1 0.0 copy-done.5
  430.1 6.7 %fusion.4 = f32[512,3584]{1,0:T(8,128)} fusion(bf16[1,3584,1024]{2,1,0:T(8,128)(2,1)S(1)} %bitcast.88, f32[512,1024]{1,0:T(8,128)S(1)} %fusion, f32[512,1024]{1,0:T(8,128)S(1)} %copy-done.5), kind=kOutput, calls=%fused_computation.10 | convolution fusion | flops 3761242112 | bytes 18874368 | tf_op jit(solution)/shard_map/dot_general | solution.py:65
  436.9 10.7 %add_convert_fusion = bf16[512,3584]{1,0:T(8,128)(2,1)S(1)} fusion(f32[512,3584]{1,0:T(8,128)} %fusion.4, bf16[1,3584,1024]{2,1,0:T(8,128)(2,1)} %param.17, f32[512,1024]{1,0:T(8,128)} %copy-done.6, f32[512,1024]{1,0:T(8,128)} %fusion.8, f32[512,1024]{1,0:T(8,128)S(1)} %copy-done.5), kind=kOutput, calls=%fused_computation.22 | convolution fusion | flops 3767009280 | bytes 24641536 | tf_op jit(solution)/shard_map/dot_general | solution.py:62
  447.6 86.4 %all_to_all.27 = bf16[16,32,3584]{2,1,0:T(8,128)(2,1)} all-to-all(bf16[16,32,3584]{2,1,0:T(8,128)(2,1)S(1)} %bitcast.83), channel_id=1, replica_groups=mesh['group'=2,'expert'=16] {'expert'}, dimensions={0} | all-to-all | bytes 7340032 | tf_op jit(solution)/shard_map/all_to_all | solution.py:69
  534.0 9.4 %gather_fusion.4 = bf16[384,3584]{1,0:T(8,128)(2,1)S(1)} fusion(bf16[512,3584]{1,0:T(8,128)(2,1)} %bitcast.75, s32[1024]{0:T(1024)S(1)} %pad_clamp_fusion), kind=kCustom, calls=%fused_computation.4.clone | custom fusion | bytes 5506560 | tf_op jit(solution)/shard_map/jit(_take)/gather | solution.py:31
  543.4 2.9 fusion.21
  546.3 0.0 copy-done
  546.3 0.0 copy-start.2
  546.3 0.3 convolution_bitcast_fusion
  546.6 1.8 copy.21
  548.4 0.0 reduce-scatter.4.cloned.1.call-update
  548.4 61.2 %reduce-scatter.4.cloned.1.call-done = f32[224,16]{1,0:T(8,128)} async-done(((f32[3584,16]{1,0:T(8,128)}), f32[224,16]{1,0:T(8,128)}) %reduce-scatter.4.cloned.1.call-update) | async-done | bytes 14352
  609.6 1.6 copy.22
  611.2 0.0 copy-done.2
  (11 shorter events, 0.1 us)
Async XLA Ops:
  7.2 539.1 %copy-start = (f32[48,16]{0,1:T(8,128)S(1)}, f32[48,16]{0,1:T(8,128)}, u32[]{:S(2)}) copy-start(f32[48,16]{0,1:T(8,128)} %param.16) | copy-start | bytes 9220
  116.7 74.4 %all-to-all-start.1 = ((bf16[16,32,3584]{2,1,0:T(8,128)(2,1)}), bf16[16,32,3584]{2,1,0:T(8,128)(2,1)}, u32[]{:S(2)}, u32[]{:S(2)}) async-start(bf16[16,32,3584]{2,1,0:T(8,128)(2,1)} %bitcast.76), calls=%async_computation.1 | async-start | bytes 7340032 | tf_op jit(solution)/shard_map/all_to_all | solution.py:35
  122.5 7.5 %copy-start.1 = (bf16[16,32,3584]{2,1,0:T(8,128)(2,1)S(1)}, bf16[16,32,3584]{2,1,0:T(8,128)(2,1)}, u32[]{:S(2)}) copy-start(bf16[16,32,3584]{2,1,0:T(8,128)(2,1)} %all_to_all.25) | copy-start | bytes 11010052
  130.0 70.6 %copy-start.4 = (f32[512,1024]{1,0:T(8,128)}, f32[512,1024]{1,0:T(8,128)S(1)}, u32[]{:S(2)}) copy-start(f32[512,1024]{1,0:T(8,128)S(1)} %fusion.14) | copy-start | bytes 6291460
  218.4 17.9 %copy-start.3 = (f32[48,8]{0,1:T(8,128)S(1)}, f32[48,8]{0,1:T(8,128)}, u32[]{:S(2)}) copy-start(f32[48,8]{0,1:T(8,128)} %param.15) | copy-start | bytes 4612
  218.4 86.3 %all-to-all-start.2 = ((bf16[16,32,3584]{2,1,0:T(8,128)(2,1)}), bf16[16,32,3584]{2,1,0:T(8,128)(2,1)}, u32[]{:S(2)}, u32[]{:S(2)}) async-start(bf16[16,32,3584]{2,1,0:T(8,128)(2,1)} %bitcast.80), calls=%async_computation.2 | async-start | bytes 7340032 | tf_op jit(solution)/shard_map/all_to_all | solution.py:49
  236.1 373.5 %reduce-scatter.4.cloned.1.call-start = ((), (), s32[]{:S(2)}) async-start(), calls=%async_computation.6 | async-start | bytes 1949696
  323.5 106.6 %slice-start = ((s8[7340032]{0:T(1024)(128)(4,1)}), s8[4194304]{0:T(1024)(128)(4,1)S(1)}, s32[]{:S(2)}) async-start(s8[7340032]{0:T(1024)(128)(4,1)} %bitcast.87), calls=%async_computation.7 | async-start | bytes 8388608
  422.4 7.7 %slice-start.1 = ((s8[7340032]{0:T(1024)(128)(4,1)}), s8[3145728]{0:T(1024)(128)(4,1)S(1)}, s32[]{:S(2)}) async-start(s8[7340032]{0:T(1024)(128)(4,1)} %bitcast.87), calls=%async_computation.8 | async-start | bytes 6291456
  422.4 7.7 %copy-start.5 = (f32[512,1024]{1,0:T(8,128)S(1)}, f32[512,1024]{1,0:T(8,128)}, u32[]{:S(2)}) copy-start(f32[512,1024]{1,0:T(8,128)} %copy-done.4) | copy-start | bytes 6291460
  428.8 1.3 copy-start.6
  546.3 64.9 %copy-start.2 = (bf16[48,3584]{1,0:T(8,128)(2,1)}, bf16[48,3584]{1,0:T(8,128)(2,1)S(1)}, u32[]{:S(2)}) copy-start(bf16[48,3584]{1,0:T(8,128)(2,1)S(1)} %fusion.21) | copy-start | bytes 1032196
Sparse Core Ops, SparseCore 0:
  548.5 61.0 reduce-scatter.3
where the time goes:
time: 623 us; the launch traced here: 618 us
  blocking collectives  274 us (44%)
  waiting for transfers between devices  182 us (29%)
  matrix products  67.2 us (11%)
  local copies, waits for them, and re-layouts  42.4 us (7%)
  starting transfers between devices  23.7 us (4%)
  other arithmetic  14.7 us (2%)
  between operations  14.5 us (2%)
    all_to_all x1, blocking collectives, body(): lax.all_to_all(spread(combined), 'expert', split_axis=0, concat_axis=0, t...  98.8 us
    all_to_all x1, blocking collectives, body(): lax.all_to_all(spread(tokens), 'expert', split_axis=0, concat_axis=0, til...  88.3 us
    all_to_all x1, blocking collectives, body(): lax.all_to_all(back, 'expert', split_axis=0, concat_axis=0, tiled=True)  86.4 us
    all_to_all x1, waiting for transfers between devices, body(): lax.all_to_all(tout.reshape(count, cap, width), 'expert', split_axis=0, c...  68.2 us
    unnamed x2, waiting for transfers between devices  61.2 us
    all_to_all x1, waiting for transfers between devices, body(): lax.all_to_all(spread(tangent), 'expert', split_axis=0, concat_axis=0, ti...  52.7 us
    gather x2, local copies, waits for them, and re-layouts, collect(): picked = jnp.take(returned.reshape(count * cap, width), place, axis=0)  18.8 us
    dot_general x1, matrix products, body(): jnp.dot(hidden, w_d, preferred_element_type=jnp.float32)  17.7 us
  transfers between devices with their start and end apart: 3, of which 3 were waited for; matrix products, arithmetic and copies ran while one was open for 3% of the time, Pallas kernels for 0%

commit v1 on v0

v1 whole, which is shorter than its diff:
```python
import functools

import jax
import jax.numpy as jnp
from jax import lax
from jax.experimental import pallas as pl
from jax.experimental.pallas import tpu as pltpu
from jax.sharding import PartitionSpec as P

BF16 = jnp.bfloat16
F32 = jnp.float32
VMEM_BYTES = 48 * 1024 * 1024


def swap(values, perm):
    return lax.ppermute(values, "expert", perm)


def mm(left, right):
    return jnp.dot(left, right, preferred_element_type=F32)


def mm_t(left, right):
    return lax.dot_general(left, right, (((1,), (1,)), ((), ())), preferred_element_type=F32)


def up_kernel(f_steps, rows, p0, p1, p2, p3, gate, w_g, w_u, w_d, keep, send, u_out, v_out, x_all, th_all, sems):
    step = pl.program_id(0)
    block = 4 * rows
    f_tile = w_g.shape[1]

    @pl.when(step == 0)
    def _():
        copies = []
        for j, piece in enumerate((p0, p1, p2, p3)):
            for part in range(2):
                copies.append(
                    pltpu.make_async_copy(
                        piece.at[pl.ds(part * rows, rows)],
                        x_all.at[pl.ds(part * block + j * rows, rows)],
                        sems.at[2 * j + part],
                    )
                )
        for copy in copies:
            copy.start()
        for copy in copies:
            copy.wait()

    @pl.when(step < f_steps)
    def _():
        x = x_all[...]
        both_a = mm(x, w_g[...])
        both_b = mm(x, w_u[...])
        a, ta = both_a[:block], both_a[block:]
        b, tb = both_b[:block], both_b[block:]
        sig = jax.nn.sigmoid(a)
        g = gate[...]
        u = (sig * (1.0 + a * (1.0 - sig))) * b * g
        v = a * sig * g
        u_out[...] = u
        v_out[...] = v
        th_all[step] = (u * ta + v * tb).astype(BF16)

    @pl.when(step >= f_steps)
    def _():
        out = mm(th_all[0], w_d[pl.ds(0, f_tile), :])
        for k in range(1, f_steps):
            out = out + mm(th_all[k], w_d[pl.ds(k * f_tile, f_tile), :])
        out = out.astype(BF16)
        keep[...] = out[: 2 * rows]
        send[...] = out[2 * rows :]


def down_kernel(f_steps, rows, p0, p1, p2, p3, u_in, v_in, w_d, w_g, w_u, keep, send, x_all, ga_all, gb_all, sems):
    step = pl.program_id(0)
    f_tile = w_d.shape[0]

    @pl.when(step == 0)
    def _():
        copies = []
        for j, piece in enumerate((p0, p1, p2, p3)):
            copies.append(pltpu.make_async_copy(piece, x_all.at[pl.ds(j * rows, rows)], sems.at[j]))
        for copy in copies:
            copy.start()
        for copy in copies:
            copy.wait()

    @pl.when(step < f_steps)
    def _():
        gh = mm_t(x_all[...], w_d[...])
        ga_all[step] = (gh * u_in[...]).astype(BF16)
        gb_all[step] = (gh * v_in[...]).astype(BF16)

    @pl.when(step >= f_steps)
    def _():
        out = None
        for k in range(f_steps):
            columns = pl.ds(k * f_tile, f_tile)
            term = mm_t(ga_all[k], w_g[:, columns]) + mm_t(gb_all[k], w_u[:, columns])
            out = term if out is None else out + term
        out = out.astype(BF16)
        keep[...] = out[: 2 * rows]
        send[...] = out[2 * rows :]


def tile_of(size, most):
    for tile in range(min(size, most), 0, -128):
        if size % tile == 0 and tile % 128 == 0:
            return tile
    return size


def up_call(pieces, gate, w_g, w_u, w_d):
    width, hidden = w_g.shape
    rows = pieces[0].shape[0] // 2
    f_tile, d_tile = tile_of(hidden, 256), tile_of(width, 896)
    f_steps, d_steps = hidden // f_tile, width // d_tile
    first = lambda i: jnp.minimum(i, f_steps - 1)
    second = lambda i: jnp.maximum(i - f_steps, 0)
    block = 4 * rows
    flops = 2 * width * hidden * block * 5
    return pl.pallas_call(
        functools.partial(up_kernel, f_steps, rows),
        grid=(f_steps + d_steps,),
        in_specs=[pl.BlockSpec(memory_space=pl.ANY)] * 4
        + [
            pl.BlockSpec((block, 1), lambda i: (0, 0)),
            pl.BlockSpec((width, f_tile), lambda i: (0, first(i))),
            pl.BlockSpec((width, f_tile), lambda i: (0, first(i))),
            pl.BlockSpec((hidden, d_tile), lambda i: (0, second(i))),
        ],
        out_specs=[
            pl.BlockSpec((2 * rows, d_tile), lambda i: (0, second(i))),
            pl.BlockSpec((2 * rows, d_tile), lambda i: (0, second(i))),
            pl.BlockSpec((block, f_tile), lambda i: (0, first(i))),
            pl.BlockSpec((block, f_tile), lambda i: (0, first(i))),
        ],
        out_shape=[
            jax.ShapeDtypeStruct((2 * rows, width), BF16),
            jax.ShapeDtypeStruct((2 * rows, width), BF16),
            jax.ShapeDtypeStruct((block, hidden), F32),
            jax.ShapeDtypeStruct((block, hidden), F32),
        ],
        scratch_shapes=[
            pltpu.VMEM((2 * block, width), BF16),
            pltpu.VMEM((f_steps, block, f_tile), BF16),
            pltpu.SemaphoreType.DMA((8,)),
        ],
        compiler_params=pltpu.CompilerParams(vmem_limit_bytes=VMEM_BYTES),
        cost_estimate=pl.CostEstimate(flops=flops, bytes_accessed=6 * width * hidden, transcendentals=0),
    )(*pieces, gate, w_g, w_u, w_d)


def down_call(pieces, u, v, w_g, w_u, w_d):
    width, hidden = w_g.shape
    rows = pieces[0].shape[0]
    f_tile, d_tile = tile_of(hidden, 256), tile_of(width, 896)
    f_steps, d_steps = hidden // f_tile, width // d_tile
    first = lambda i: jnp.minimum(i, f_steps - 1)
    second = lambda i: jnp.maximum(i - f_steps, 0)
    block = 4 * rows
    flops = 2 * width * hidden * block * 3
    return pl.pallas_call(
        functools.partial(down_kernel, f_steps, rows),
        grid=(f_steps + d_steps,),
        in_specs=[pl.BlockSpec(memory_space=pl.ANY)] * 4
        + [
            pl.BlockSpec((block, f_tile), lambda i: (0, first(i))),
            pl.BlockSpec((block, f_tile), lambda i: (0, first(i))),
            pl.BlockSpec((f_tile, width), lambda i: (first(i), 0)),
            pl.BlockSpec((d_tile, hidden), lambda i: (second(i), 0)),
            pl.BlockSpec((d_tile, hidden), lambda i: (second(i), 0)),
        ],
        out_specs=[
            pl.BlockSpec((2 * rows, d_tile), lambda i: (0, second(i))),
            pl.BlockSpec((2 * rows, d_tile), lambda i: (0, second(i))),
        ],
        out_shape=[
            jax.ShapeDtypeStruct((2 * rows, width), BF16),
            jax.ShapeDtypeStruct((2 * rows, width), BF16),
        ],
        scratch_shapes=[
            pltpu.VMEM((block, width), BF16),
            pltpu.VMEM((f_steps, block, f_tile), BF16),
            pltpu.VMEM((f_steps, block, f_tile), BF16),
            pltpu.SemaphoreType.DMA((4,)),
        ],
        compiler_params=pltpu.CompilerParams(vmem_limit_bytes=VMEM_BYTES),
        cost_estimate=pl.CostEstimate(flops=flops, bytes_accessed=6 * width * hidden, transcendentals=0),
    )(*pieces, u, v, w_d, w_g, w_u)


def gather_blocks(own, ring, across, pair):
    depth = len(ring) // 4
    blocks, held = [], own
    for s in range(depth):
        other = swap(held, across)
        blocks.append((held, other, swap(held, pair), swap(other, pair)))
        if s < depth - 1:
            held = swap(held, ring)
    return blocks


def scatter_sum(halves, ring, across, pair):
    depth = len(halves)
    rows = halves[0][0].shape[0] // 2
    moving = None
    for s in list(range(1, depth)) + [0]:
        keep, send = halves[s]
        got = swap(send, pair)
        far = (keep[rows:].astype(F32) + got[rows:].astype(F32)).astype(BF16)
        total = keep[:rows].astype(F32) + got[:rows].astype(F32) + swap(far, across).astype(F32)
        if moving is not None:
            total = total + moving.astype(F32)
        if s:
            moving = swap(total.astype(BF16), ring)
    return total.astype(BF16)


def body(tokens, tangent, routes, gates, probes, w_gate, w_up, w_down):
    rows, width = tokens.shape
    count = lax.axis_size("expert")
    depth = count // 4
    ring = [(i, (i + 4) % count) for i in range(count)]
    across = [(i, i ^ 2) for i in range(count)]
    pair = [(i, i ^ 1) for i in range(count)]
    w_g, w_u, w_d = w_gate[0], w_up[0], w_down[0]
    me = lax.axis_index("expert")

    experts = jnp.arange(count, dtype=jnp.int32)
    hit = routes[None, :, :] == experts[:, None, None]
    dense = jnp.sum(jnp.where(hit, gates[None], 0.0), axis=2)
    dense = lax.all_to_all(dense, "expert", split_axis=0, concat_axis=0, tiled=True)
    order = jnp.arange(count, dtype=jnp.int32)
    flip = jnp.array([0, 2, 1, 3], jnp.int32)[order % 4]
    source = ((me // 4 - order // 4 + depth) % depth) * 4 + ((me % 4) ^ flip)
    dense = jnp.take(dense, source, axis=0).reshape(depth, 4 * rows, 1)

    stacked = jnp.concatenate([tokens, tangent], axis=0)
    blocks = gather_blocks(stacked, ring, across, pair)
    halves, saved = [], []
    for s in range(depth):
        keep, send, u, v = up_call(blocks[s], dense[s], w_g, w_u, w_d)
        halves.append((keep, send))
        saved.append((u, v))
    combined = scatter_sum(halves, ring, across, pair)
    blocks = gather_blocks(combined, ring, across, pair)
    halves = [down_call(blocks[s], *saved[s], w_g, w_u, w_d) for s in range(depth)]
    curvature_rows = scatter_sum(halves, ring, across, pair)
    term = lax.dot_general(
        probes,
        curvature_rows.astype(F32),
        (((0,), (0,)), ((), ())),
        precision=lax.Precision.HIGHEST,
        preferred_element_type=F32,
    )
    share = width // count
    rank = term.shape[0]
    term = term.reshape(rank, count, share).transpose(1, 0, 2)
    term = lax.all_to_all(term, "expert", split_axis=0, concat_axis=0, tiled=True)
    sketch = jnp.sum(term, axis=0)
    return (curvature_rows, sketch)


def solution(mesh):
    return jax.shard_map(
        body,
        mesh=mesh,
        in_specs=(
            P(("group", "expert"), None),
            P(("group", "expert"), None),
            P(("group", "expert"), None),
            P(("group", "expert"), None),
            P(("group", "expert"), None),
            P("expert", None, None),
            P("expert", None, None),
            P("expert", None, None),
        ),
        out_specs=(P(("group", "expert"), None), P("group", "expert")),
        check_vma=False,
    )
```

time: 623 us -> 294 us (0.47)
  blocking collectives: 274 us -> 12.7 us
  Pallas kernels: 0 us -> 121 us
  waiting for transfers between devices: 182 us -> 105 us
  matrix products: 67.2 us -> 0.26 us
  local copies, waits for them, and re-layouts: 42.4 us -> 9.7 us
  between operations: 14.5 us -> 1.07 us
  starting transfers between devices: 23.7 us -> 37.1 us
  other arithmetic: 14.7 us -> 5.99 us
    all_to_all x3 -> x1, blocking collectives: 274 us -> 12.7 us  [body(): lax.all_to_all(term, 'expert', split_axis=0, concat_axis=0, tiled=True)]
    pallas_call x0 -> x8, Pallas kernels: none -> 121 us  [the longest x4 64.5 us: up_call(): pl.pallas_call(functools.partial(up_kernel, f_steps, rows), grid=(f_steps...]
    all_to_all x2 -> x1, waiting for transfers between devices: 121 us -> 12.2 us  [body(): lax.all_to_all(dense, 'expert', split_axis=0, concat_axis=0, tiled=True)]
    ppermute x0 -> x52, waiting for transfers between devices: none -> 92.8 us  [swap(): return lax.ppermute(values, 'expert', perm)]
    dot_general x8 -> x1, matrix products: 67.2 us -> 0.26 us  [body(): lax.dot_general(probes, curvature_rows.astype(F32), (((0,), (0,)), ((), (...]
    unnamed x2 -> x0, waiting for transfers between devices: 61.2 us -> none
    ppermute x0 -> x52, starting transfers between devices: none -> 32.9 us  [swap(): return lax.ppermute(values, 'expert', perm)]
    gather x5 -> x2, local copies, waits for them, and re-layouts: 31.3 us -> 1.88 us  [the longest x1 1.32 us: body(): flip = jnp.array([0, 2, 1, 3], jnp.int32)[order % 4]]
  transfers between devices with their start and end apart: 3 -> 53, of which waited for: 3 -> 22; matrix products, arithmetic and copies ran while one was open for 3% -> 3% of each run, Pallas kernels for 0% -> 41%
where the time goes in v1:
time: 294 us; the launch traced here: 293 us
  Pallas kernels  121 us (41%)
  waiting for transfers between devices  105 us (36%)
  starting transfers between devices  37.1 us (13%)
  blocking collectives  12.7 us (4%)
  local copies, waits for them, and re-layouts  9.7 us (3%)
  other arithmetic  5.99 us (2%)
    ppermute x52, waiting for transfers between devices, swap(): return lax.ppermute(values, 'expert', perm)  92.8 us
    pallas_call x4, Pallas kernels, up_call(): pl.pallas_call(functools.partial(up_kernel, f_steps, rows), grid=(f_steps...  64.5 us
    pallas_call x4, Pallas kernels, down_call(): pl.pallas_call(functools.partial(down_kernel, f_steps, rows), grid=(f_ste...  56.7 us
    ppermute x52, starting transfers between devices, swap(): return lax.ppermute(values, 'expert', perm)  32.9 us
    all_to_all x1, blocking collectives, body(): lax.all_to_all(term, 'expert', split_axis=0, concat_axis=0, tiled=True)  12.7 us
    all_to_all x1, waiting for transfers between devices, body(): lax.all_to_all(dense, 'expert', split_axis=0, concat_axis=0, tiled=True)  12.2 us
    unnamed x17, local copies, waits for them, and re-layouts  6.01 us
  transfers between devices with their start and end apart: 53, of which 22 were waited for; matrix products, arithmetic and copies ran while one was open for 3% of the time, Pallas kernels for 41%

profile of v1, /device:TPU:0, one launch (start us, length us, event | category | flops | bytes accessed | tf_op | source)
XLA Modules:
  0.0 292.9 jit_solution(10222502213260886171)
XLA Ops:
  0.6 1.0 constant_dynamic-update-slice_fusion.1
  1.7 1.0 constant_dynamic-update-slice_fusion.p0
  2.7 3.1 %collective-permute-start.5 = (bf16[96,3584]{1,0:T(8,128)(2,1)S(1)}, bf16[96,3584]{1,0:T(8,128)(2,1)S(1)}, u32[]{:S(2)}, u32[]{:S(2)}) collective-permute-start(bf16[96,3584]{1,0:T(8,128)(2,1)S(1)} %constant_dynamic-update-slice_fusion.p0), channel_id=1, source_target_pairs={{0,4},{1,5},{2,6},{3,7},{4,8},{5,9},{6,10},{7,11},{8,12},{9,13},{1... | collective-permute-start | bytes 2064392 | tf_op jit(solution)/shard_map/ppermute | solution.py:16
  5.7 17.5 %collective-permute-done.5.p0 = bf16[96,3584]{1,0:T(8,128)(2,1)S(1)} collective-permute-done((bf16[96,3584]{1,0:T(8,128)(2,1)S(1)}, bf16[96,3584]{1,0:T(8,128)(2,1)S(1)}, u32[]{:S(2)}, u32[]{:S(2)}) %collective-permute-start.5) | collective-permute-done | bytes 688160 | tf_op jit(solution)/shard_map/ppermute | solution.py:16
  23.2 1.5 collective-permute-start.18
  25.2 1.3 select_reduce_fusion
  26.6 4.2 %all-to-all-start = ((f32[16,1,48]{2,1,0:T(1,128)}), f32[16,1,48]{2,1,0:T(1,128)S(1)}, u32[]{:S(2)}, u32[]{:S(2)}) async-start(f32[16,1,48]{2,1,0:T(1,128)} %bitcast.2), calls=%async_computation | async-start | bytes 16384 | tf_op jit(solution)/shard_map/all_to_all | solution.py:233
  30.8 1.3 gather_fusion
  32.6 1.7 collective-permute-start.6
  34.3 7.4 %collective-permute-done.18.p1 = bf16[96,3584]{1,0:T(8,128)(2,1)S(1)} collective-permute-done((bf16[96,3584]{1,0:T(8,128)(2,1)S(1)}, bf16[96,3584]{1,0:T(8,128)(2,1)S(1)}, u32[]{:S(2)}, u32[]{:S(2)}) %collective-permute-start.18) | collective-permute-done | bytes 688160 | tf_op jit(solution)/shard_map/ppermute | solution.py:16
  41.6 0.9 copy-done.3
  42.5 12.2 %all-to-all-done = f32[16,1,48]{2,1,0:T(1,128)S(1)} async-done(((f32[16,1,48]{2,1,0:T(1,128)}), f32[16,1,48]{2,1,0:T(1,128)S(1)}, u32[]{:S(2)}, u32[]{:S(2)}) %all-to-all-start) | async-done | bytes 3104 | tf_op jit(solution)/shard_map/all_to_all | solution.py:233
  54.8 0.6 gather_fusion.1
  55.7 1.3 collective-permute-start.13
  57.0 0.8 copy-done.5
  57.8 1.1 copy-done.2
  58.9 1.1 copy-done.4
  60.0 1.1 copy-done.6
  61.1 16.8 %shard_map.107 = (bf16[96,3584]{1,0:T(8,128)(2,1)S(1)}, bf16[96,3584]{1,0:T(8,128)(2,1)}, f32[192,1024]{1,0:T(8,128)S(1)}, f32[192,1024]{1,0:T(8,128)S(1)}) custom-call(bf16[96,3584]{1,0:T(8,128)(2,1)S(1)} %copy-done.2, bf16[96,3584]{1,0:T(8,128)(2,1)S(1)} %copy-done.4, bf16[96,3584]{1,0:T(8,128)(2,1)S(1)} %copy-done.6, ...), custom_call_target="tpu_custom_call" | custom-call | flops 7046430720 | bytes 22020096 | tf_op jit(solution)/shard_map/pallas_call | solution.py:122
  78.5 16.2 %shard_map.104 = (bf16[96,3584]{1,0:T(8,128)(2,1)S(1)}, bf16[96,3584]{1,0:T(8,128)(2,1)S(1)}, f32[192,1024]{1,0:T(8,128)S(1)}, f32[192,1024]{1,0:T(8,128)S(1)}) custom-call(bf16[96,3584]{1,0:T(8,128)(2,1)S(1)} %constant_dynamic-update-slice_fusion.p0, bf16[96,3584]{1,0:T(8,128)(2,1)} %collective-permute-done.p1, bf16[96,3584]{1,0:T(8,128)(2,1)} %collective-permute-done.1.p2, ...), custom_call_target="tpu_custom_call" | custom-call | flops 7046430720 | bytes 22020096 | tf_op jit(solution)/shard_map/pallas_call | solution.py:122
  95.3 0.7 collective-permute-start.8
  96.6 1.1 add_convert_fusion.12
  98.1 0.9 collective-permute-start.22
  99.0 1.1 collective-permute-done.15.p3
  100.1 15.8 %shard_map.106 = (bf16[96,3584]{1,0:T(8,128)(2,1)S(1)}, bf16[96,3584]{1,0:T(8,128)(2,1)S(1)}, f32[192,1024]{1,0:T(8,128)S(1)}, f32[192,1024]{1,0:T(8,128)S(1)}) custom-call(bf16[96,3584]{1,0:T(8,128)(2,1)} %collective-permute-done.6.p0, bf16[96,3584]{1,0:T(8,128)(2,1)} %collective-permute-done.13.p1, bf16[96,3584]{1,0:T(8,128)(2,1)S(1)} %collective-permute-done.14.p2, ...), custom_call_target="tpu_custom_call" | custom-call | flops 7046430720 | bytes 22020096 | tf_op jit(solution)/shard_map/pallas_call | solution.py:122
  116.5 4.1 %collective-permute-done.22 = bf16[48,3584]{1,0:T(8,128)(2,1)S(1)} collective-permute-done((bf16[48,3584]{1,0:T(8,128)(2,1)S(1)}, bf16[48,3584]{1,0:T(8,128)(2,1)S(1)}, u32[]{:S(2)}, u32[]{:S(2)}) %collective-permute-start.22) | collective-permute-done | bytes 344096 | tf_op jit(solution)/shard_map/ppermute | solution.py:16
  120.6 1.1 add_convert_fusion.11
  121.7 1.3 collective-permute-start.23
  123.1 0.6 collective-permute-start.17
  123.7 15.6 %shard_map.105 = (bf16[96,3584]{1,0:T(8,128)(2,1)S(1)}, bf16[96,3584]{1,0:T(8,128)(2,1)S(1)}, f32[192,1024]{1,0:T(8,128)S(1)}, f32[192,1024]{1,0:T(8,128)S(1)}) custom-call(bf16[96,3584]{1,0:T(8,128)(2,1)} %collective-permute-done.7.p0, bf16[96,3584]{1,0:T(8,128)(2,1)S(1)} %collective-permute-done.8.p1, bf16[96,3584]{1,0:T(8,128)(2,1)S(1)} %collective-permute-done.9.p2, ...), custom_call_target="tpu_custom_call" | custom-call | flops 7046430720 | bytes 22020096 | tf_op jit(solution)/shard_map/pallas_call | solution.py:122
  139.6 1.6 collective-permute-start.24
  141.6 1.6 collective-permute-start.12
  143.3 0.6 collective-permute-start.4
  143.9 8.0 %collective-permute-done.24 = bf16[48,3584]{1,0:T(8,128)(2,1)S(1)} collective-permute-done((bf16[48,3584]{1,0:T(8,128)(2,1)S(1)}, bf16[48,3584]{1,0:T(8,128)(2,1)S(1)}, u32[]{:S(2)}, u32[]{:S(2)}) %collective-permute-start.24) | collective-permute-done | bytes 344096 | tf_op jit(solution)/shard_map/ppermute | solution.py:16
  151.9 0.7 collective-permute-done.12
  152.8 2.1 collective-permute-start.25
  154.9 4.3 %collective-permute-done.4 = bf16[48,3584]{1,0:T(8,128)(2,1)S(1)} collective-permute-done((bf16[48,3584]{1,0:T(8,128)(2,1)S(1)}, bf16[48,3584]{1,0:T(8,128)(2,1)S(1)}, u32[]{:S(2)}, u32[]{:S(2)}) %collective-permute-start.4) | collective-permute-done | bytes 344096 | tf_op jit(solution)/shard_map/ppermute | solution.py:16
  159.2 4.4 %collective-permute-done.25 = bf16[48,3584]{1,0:T(8,128)(2,1)S(1)} collective-permute-done((bf16[48,3584]{1,0:T(8,128)(2,1)S(1)}, bf16[48,3584]{1,0:T(8,128)(2,1)S(1)}, u32[]{:S(2)}, u32[]{:S(2)}) %collective-permute-start.25) | collective-permute-done | bytes 344096 | tf_op jit(solution)/shard_map/ppermute | solution.py:16
  163.8 9.8 %collective-permute-done.31.p0 = bf16[48,3584]{1,0:T(8,128)(2,1)S(1)} collective-permute-done((bf16[48,3584]{1,0:T(8,128)(2,1)S(1)}, bf16[48,3584]{1,0:T(8,128)(2,1)S(1)}, u32[]{:S(2)}, u32[]{:S(2)}) %collective-permute-start.31) | collective-permute-done | bytes 344096 | tf_op jit(solution)/shard_map/ppermute | solution.py:16
  173.7 1.5 collective-permute-start.44
  175.2 0.5 collective-permute-start.26
  175.7 8.8 %collective-permute-done.44.p1 = bf16[48,3584]{1,0:T(8,128)(2,1)S(1)} collective-permute-done((bf16[48,3584]{1,0:T(8,128)(2,1)S(1)}, bf16[48,3584]{1,0:T(8,128)(2,1)S(1)}, u32[]{:S(2)}, u32[]{:S(2)}) %collective-permute-start.44) | collective-permute-done | bytes 344096 | tf_op jit(solution)/shard_map/ppermute | solution.py:16
  184.5 0.5 collective-permute-start.27
  185.0 3.2 %collective-permute-done.26.p1 = bf16[48,3584]{1,0:T(8,128)(2,1)S(1)} collective-permute-done((bf16[48,3584]{1,0:T(8,128)(2,1)S(1)}, bf16[48,3584]{1,0:T(8,128)(2,1)S(1)}, u32[]{:S(2)}, u32[]{:S(2)}) %collective-permute-start.26) | collective-permute-done | bytes 344096 | tf_op jit(solution)/shard_map/ppermute | solution.py:16
  188.2 14.2 %shard_map.111 = (bf16[96,3584]{1,0:T(8,128)(2,1)S(1)}, bf16[96,3584]{1,0:T(8,128)(2,1)S(1)}) custom-call(bf16[48,3584]{1,0:T(8,128)(2,1)S(1)} %collective-permute-done.31.p0, bf16[48,3584]{1,0:T(8,128)(2,1)S(1)} %collective-permute-done.44.p1, bf16[48,3584]{1,0:T(8,128)(2,1)S(1)} %collective-permute-done.45.p2, ...), custom_call_target="tpu_custom_call" | custom-call | flops 4227858432 | bytes 22020096 | tf_op jit(solution)/shard_map/pallas_call | solution.py:163
  202.4 0.6 collective-permute-start.47
  202.9 1.5 collective-permute-start.39
  204.4 14.2 %shard_map.108 = (bf16[96,3584]{1,0:T(8,128)(2,1)S(1)}, bf16[96,3584]{1,0:T(8,128)(2,1)S(1)}) custom-call(bf16[48,3584]{1,0:T(8,128)(2,1)S(1)} %add_convert_fusion.8.p0, bf16[48,3584]{1,0:T(8,128)(2,1)S(1)} %collective-permute-done.26.p1, bf16[48,3584]{1,0:T(8,128)(2,1)S(1)} %collective-permute-done.27.p2, bf16[48,3584]{1,0:T(8,128)(2,1)S(1)} %collective-permute-done.28.p3, ...), custom_call_target="tpu_custom_call" | custom-call | flops 4227858432 | bytes 22020096 | tf_op jit(solution)/shard_map/pallas_call | solution.py:163
  219.2 0.5 collective-permute-start.34
  220.3 1.0 collective-permute-done.40.p2
  221.3 0.6 collective-permute-start.48
  222.3 14.1 %shard_map.110 = (bf16[96,3584]{1,0:T(8,128)(2,1)S(1)}, bf16[96,3584]{1,0:T(8,128)(2,1)S(1)}) custom-call(bf16[48,3584]{1,0:T(8,128)(2,1)S(1)} %collective-permute-done.32.p0, bf16[48,3584]{1,0:T(8,128)(2,1)S(1)} %collective-permute-done.39.p1, bf16[48,3584]{1,0:T(8,128)(2,1)S(1)} %collective-permute-done.40.p2, ...), custom_call_target="tpu_custom_call" | custom-call | flops 4227858432 | bytes 22020096 | tf_op jit(solution)/shard_map/pallas_call | solution.py:163
  237.2 1.4 collective-permute-done.42
  238.8 1.1 collective-permute-start.43
  239.9 14.2 %shard_map.109 = (bf16[96,3584]{1,0:T(8,128)(2,1)S(1)}, bf16[96,3584]{1,0:T(8,128)(2,1)S(1)}) custom-call(bf16[48,3584]{1,0:T(8,128)(2,1)S(1)} %collective-permute-done.33.p0, bf16[48,3584]{1,0:T(8,128)(2,1)S(1)} %collective-permute-done.34.p1, bf16[48,3584]{1,0:T(8,128)(2,1)S(1)} %collective-permute-done.35.p2, ...), custom_call_target="tpu_custom_call" | custom-call | flops 4227858432 | bytes 22020096 | tf_op jit(solution)/shard_map/pallas_call | solution.py:163
  254.7 1.6 collective-permute-done.37
  256.4 1.0 collective-permute-start.38
  257.5 1.1 collective-permute-start.30
  258.6 8.3 %collective-permute-done.50 = bf16[48,3584]{1,0:T(8,128)(2,1)S(1)} collective-permute-done((bf16[48,3584]{1,0:T(8,128)(2,1)S(1)}, bf16[48,3584]{1,0:T(8,128)(2,1)S(1)}, u32[]{:S(2)}, u32[]{:S(2)}) %collective-permute-start.50) | collective-permute-done | bytes 344096 | tf_op jit(solution)/shard_map/ppermute | solution.py:16
  267.5 1.7 collective-permute-start.51
  269.2 4.7 %collective-permute-done.30 = bf16[48,3584]{1,0:T(8,128)(2,1)S(1)} collective-permute-done((bf16[48,3584]{1,0:T(8,128)(2,1)S(1)}, bf16[48,3584]{1,0:T(8,128)(2,1)S(1)}, u32[]{:S(2)}, u32[]{:S(2)}) %collective-permute-start.30) | collective-permute-done | bytes 344096 | tf_op jit(solution)/shard_map/ppermute | solution.py:16
  273.9 4.9 %collective-permute-done.51 = bf16[48,3584]{1,0:T(8,128)(2,1)S(1)} collective-permute-done((bf16[48,3584]{1,0:T(8,128)(2,1)S(1)}, bf16[48,3584]{1,0:T(8,128)(2,1)S(1)}, u32[]{:S(2)}, u32[]{:S(2)}) %collective-permute-start.51) | collective-permute-done | bytes 344096 | tf_op jit(solution)/shard_map/ppermute | solution.py:16
  279.6 12.7 %all_to_all.17 = f32[16,16,224]{2,1,0:T(8,128)S(1)} all-to-all(f32[16,16,224]{2,1,0:T(8,128)S(1)} %bitcast.46), channel_id=1, replica_groups=mesh['group'=2,'expert'=16] {'expert'}, dimensions={0} | all-to-all | bytes 458752 | tf_op jit(solution)/shard_map/all_to_all | solution.py:260
  292.3 0.6 reduce_sum.19
  (103 shorter events, 10.0 us)
Async XLA Ops:
  0.6 278.3 %copy-start = (f32[48,16]{0,1:T(8,128)S(1)}, f32[48,16]{0,1:T(8,128)}, u32[]{:S(2)}) copy-start(f32[48,16]{0,1:T(8,128)} %param.13) | copy-start | bytes 9220
  2.7 20.5 %collective-permute-start.5 = (bf16[96,3584]{1,0:T(8,128)(2,1)S(1)}, bf16[96,3584]{1,0:T(8,128)(2,1)S(1)}, u32[]{:S(2)}, u32[]{:S(2)}) collective-permute-start(bf16[96,3584]{1,0:T(8,128)(2,1)S(1)} %constant_dynamic-update-slice_fusion.p0), channel_id=1, source_target_pairs={{0,4},{1,5},{2,6},{3,7},{4,8},{5,9},{6,10},{7,11},{8,12},{9,13},{1... | collective-permute-start | bytes 2064392 | tf_op jit(solution)/shard_map/ppermute | solution.py:16
  23.2 34.6 %copy-start.1 = (bf16[96,3584]{1,0:T(8,128)(2,1)}, bf16[96,3584]{1,0:T(8,128)(2,1)S(1)}, u32[]{:S(2)}) copy-start(bf16[96,3584]{1,0:T(8,128)(2,1)S(1)} %collective-permute-done.5.p0) | copy-start | bytes 2064388
  23.2 18.4 %collective-permute-start.18 = (bf16[96,3584]{1,0:T(8,128)(2,1)S(1)}, bf16[96,3584]{1,0:T(8,128)(2,1)S(1)}, u32[]{:S(2)}, u32[]{:S(2)}) collective-permute-start(bf16[96,3584]{1,0:T(8,128)(2,1)S(1)} %collective-permute-done.5.p0), channel_id=1, source_target_pairs={{0,2},{1,3},{2,0},{3,1},{4,6},{5,7},{6,4},{7,5},{8,10},{9,11},{10,... | collective-permute-start | bytes 2064392 | tf_op jit(solution)/shard_map/ppermute | solution.py:16
  24.7 30.8 %collective-permute-start = (bf16[96,3584]{1,0:T(8,128)(2,1)S(1)}, bf16[96,3584]{1,0:T(8,128)(2,1)}, u32[]{:S(2)}, u32[]{:S(2)}) collective-permute-start(bf16[96,3584]{1,0:T(8,128)(2,1)S(1)} %constant_dynamic-update-slice_fusion.p0), channel_id=1, source_target_pairs={{0,2},{1,3},{2,0},{3,1},{4,6},{5,7},{6,4},{7,5},{8,10},{9,11},{10,... | collective-permute-start | bytes 2064392 | tf_op jit(solution)/shard_map/ppermute | solution.py:16
  25.2 53.3 %collective-permute-start.1 = (bf16[96,3584]{1,0:T(8,128)(2,1)S(1)}, bf16[96,3584]{1,0:T(8,128)(2,1)}, u32[]{:S(2)}, u32[]{:S(2)}) collective-permute-start(bf16[96,3584]{1,0:T(8,128)(2,1)S(1)} %constant_dynamic-update-slice_fusion.p0), channel_id=1, source_target_pairs={{0,1},{1,0},{2,3},{3,2},{4,5},{5,4},{6,7},{7,6},{8,9},{9,8},{10,11... | collective-permute-start | bytes 2064392 | tf_op jit(solution)/shard_map/ppermute | solution.py:16
  26.6 28.2 %all-to-all-start = ((f32[16,1,48]{2,1,0:T(1,128)}), f32[16,1,48]{2,1,0:T(1,128)S(1)}, u32[]{:S(2)}, u32[]{:S(2)}) async-start(f32[16,1,48]{2,1,0:T(1,128)} %bitcast.2), calls=%async_computation | async-start | bytes 16384 | tf_op jit(solution)/shard_map/all_to_all | solution.py:233
  32.1 24.8 %collective-permute-start.19 = (bf16[96,3584]{1,0:T(8,128)(2,1)S(1)}, bf16[96,3584]{1,0:T(8,128)(2,1)S(1)}, u32[]{:S(2)}, u32[]{:S(2)}) collective-permute-start(bf16[96,3584]{1,0:T(8,128)(2,1)S(1)} %collective-permute-done.5.p0), channel_id=1, source_target_pairs={{0,1},{1,0},{2,3},{3,2},{4,5},{5,4},{6,7},{7,6},{8,9},{9,8},{10,11... | collective-permute-start | bytes 2064392 | tf_op jit(solution)/shard_map/ppermute | solution.py:16
  32.6 23.1 %collective-permute-start.6 = (bf16[96,3584]{1,0:T(8,128)(2,1)S(1)}, bf16[96,3584]{1,0:T(8,128)(2,1)}, u32[]{:S(2)}, u32[]{:S(2)}) collective-permute-start(bf16[96,3584]{1,0:T(8,128)(2,1)S(1)} %collective-permute-done.5.p0), channel_id=1, source_target_pairs={{0,4},{1,5},{2,6},{3,7},{4,8},{5,9},{6,10},{7,11},{8,12},{9,13},{1... | collective-permute-start | bytes 2064392 | tf_op jit(solution)/shard_map/ppermute | solution.py:16
  41.6 16.2 %collective-permute-start.20 = (bf16[96,3584]{1,0:T(8,128)(2,1)S(1)}, bf16[96,3584]{1,0:T(8,128)(2,1)}, u32[]{:S(2)}, u32[]{:S(2)}) collective-permute-start(bf16[96,3584]{1,0:T(8,128)(2,1)S(1)} %collective-permute-done.18.p1), channel_id=1, source_target_pairs={{0,1},{1,0},{2,3},{3,2},{4,5},{5,4},{6,7},{7,6},{8,9},{9,8},{10,11... | collective-permute-start | bytes 2064392 | tf_op jit(solution)/shard_map/ppermute | solution.py:16
  41.6 0.9 copy-start.3
  55.5 23.0 %collective-permute-start.2 = (bf16[96,3584]{1,0:T(8,128)(2,1)}, bf16[96,3584]{1,0:T(8,128)(2,1)}, u32[]{:S(2)}, u32[]{:S(2)}) collective-permute-start(bf16[96,3584]{1,0:T(8,128)(2,1)} %collective-permute-done.p1), channel_id=1, source_target_pairs={{0,1},{1,0},{2,3},{3,2},{4,5},{5,4},{6,7},{7,6},{8,9},{9,8},{10,11... | collective-permute-start | bytes 2064392 | tf_op jit(solution)/shard_map/ppermute | solution.py:16
  55.7 40.4 %collective-permute-start.13 = (bf16[96,3584]{1,0:T(8,128)(2,1)}, bf16[96,3584]{1,0:T(8,128)(2,1)}, u32[]{:S(2)}, u32[]{:S(2)}) collective-permute-start(bf16[96,3584]{1,0:T(8,128)(2,1)} %collective-permute-done.6.p0), channel_id=1, source_target_pairs={{0,2},{1,3},{2,0},{3,1},{4,6},{5,7},{6,4},{7,5},{8,10},{9,11},{10,... | collective-permute-start | bytes 2064392 | tf_op jit(solution)/shard_map/ppermute | solution.py:16
  57.0 0.8 copy-start.5
  57.8 37.5 %collective-permute-start.7 = (bf16[96,3584]{1,0:T(8,128)(2,1)}, bf16[96,3584]{1,0:T(8,128)(2,1)}, u32[]{:S(2)}, u32[]{:S(2)}) collective-permute-start(bf16[96,3584]{1,0:T(8,128)(2,1)} %collective-permute-done.6.p0), channel_id=1, source_target_pairs={{0,4},{1,5},{2,6},{3,7},{4,8},{5,9},{6,10},{7,11},{8,12},{9,13},{1... | collective-permute-start | bytes 2064392 | tf_op jit(solution)/shard_map/ppermute | solution.py:16
  57.8 1.1 copy-start.2
  58.9 1.1 copy-start.4
  60.0 1.1 copy-start.6
  77.9 18.2 %collective-permute-start.21 = (bf16[96,3584]{1,0:T(8,128)(2,1)}, bf16[96,3584]{1,0:T(8,128)(2,1)}, u32[]{:S(2)}, u32[]{:S(2)}) collective-permute-start(bf16[96,3584]{1,0:T(8,128)(2,1)} %get-tuple-element.33), channel_id=1, source_target_pairs={{0,1},{1,0},{2,3},{3,2},{4,5},{5,4},{6,7},{7,6},{8,9},{9,8},{10,11... | collective-permute-start | bytes 2064392 | tf_op jit(solution)/shard_map/ppermute | solution.py:16
  94.7 48.4 %collective-permute-start.3 = (bf16[96,3584]{1,0:T(8,128)(2,1)S(1)}, bf16[96,3584]{1,0:T(8,128)(2,1)S(1)}, u32[]{:S(2)}, u32[]{:S(2)}) collective-permute-start(bf16[96,3584]{1,0:T(8,128)(2,1)S(1)} %get-tuple-element.27), channel_id=1, source_target_pairs={{0,1},{1,0},{2,3},{3,2},{4,5},{5,4},{6,7},{7,6},{8,9},{9,8},{10,11... | collective-permute-start | bytes 2064392 | tf_op jit(solution)/shard_map/ppermute | solution.py:16
  95.1 3.0 %collective-permute-start.14 = (bf16[96,3584]{1,0:T(8,128)(2,1)}, bf16[96,3584]{1,0:T(8,128)(2,1)S(1)}, u32[]{:S(2)}, u32[]{:S(2)}) collective-permute-start(bf16[96,3584]{1,0:T(8,128)(2,1)} %collective-permute-done.6.p0), channel_id=1, source_target_pairs={{0,1},{1,0},{2,3},{3,2},{4,5},{5,4},{6,7},{7,6},{8,9},{9,8},{10,11... | collective-permute-start | bytes 2064392 | tf_op jit(solution)/shard_map/ppermute | solution.py:16
  95.3 21.0 %collective-permute-start.8 = (bf16[96,3584]{1,0:T(8,128)(2,1)}, bf16[96,3584]{1,0:T(8,128)(2,1)S(1)}, u32[]{:S(2)}, u32[]{:S(2)}) collective-permute-start(bf16[96,3584]{1,0:T(8,128)(2,1)} %collective-permute-done.7.p0), channel_id=1, source_target_pairs={{0,2},{1,3},{2,0},{3,1},{4,6},{5,7},{6,4},{7,5},{8,10},{9,11},{10,... | collective-permute-start | bytes 2064392 | tf_op jit(solution)/shard_map/ppermute | solution.py:16
  96.1 27.6 %collective-permute-start.9 = (bf16[96,3584]{1,0:T(8,128)(2,1)}, bf16[96,3584]{1,0:T(8,128)(2,1)S(1)}, u32[]{:S(2)}, u32[]{:S(2)}) collective-permute-start(bf16[96,3584]{1,0:T(8,128)(2,1)} %collective-permute-done.7.p0), channel_id=1, source_target_pairs={{0,1},{1,0},{2,3},{3,2},{4,5},{5,4},{6,7},{7,6},{8,9},{9,8},{10,11... | collective-permute-start | bytes 2064392 | tf_op jit(solution)/shard_map/ppermute | solution.py:16
  96.1 4.0 %collective-permute-start.15 = (bf16[96,3584]{1,0:T(8,128)(2,1)}, bf16[96,3584]{1,0:T(8,128)(2,1)S(1)}, u32[]{:S(2)}, u32[]{:S(2)}) collective-permute-start(bf16[96,3584]{1,0:T(8,128)(2,1)} %collective-permute-done.13.p1), channel_id=1, source_target_pairs={{0,1},{1,0},{2,3},{3,2},{4,5},{5,4},{6,7},{7,6},{8,9},{9,8},{10,11... | collective-permute-start | bytes 2064392 | tf_op jit(solution)/shard_map/ppermute | solution.py:16
  98.1 22.4 %collective-permute-start.22 = (bf16[48,3584]{1,0:T(8,128)(2,1)S(1)}, bf16[48,3584]{1,0:T(8,128)(2,1)S(1)}, u32[]{:S(2)}, u32[]{:S(2)}) collective-permute-start(bf16[48,3584]{1,0:T(8,128)(2,1)S(1)} %add_convert_fusion.12), channel_id=1, source_target_pairs={{0,2},{1,3},{2,0},{3,1},{4,6},{5,7},{6,4},{7,5},{8,10},{9,11},{10,... | collective-permute-start | bytes 1032200 | tf_op jit(solution)/shard_map/ppermute | solution.py:16
  115.9 7.0 %collective-permute-start.16 = (bf16[96,3584]{1,0:T(8,128)(2,1)S(1)}, bf16[96,3584]{1,0:T(8,128)(2,1)S(1)}, u32[]{:S(2)}, u32[]{:S(2)}) collective-permute-start(bf16[96,3584]{1,0:T(8,128)(2,1)S(1)} %get-tuple-element.31), channel_id=1, source_target_pairs={{0,1},{1,0},{2,3},{3,2},{4,5},{5,4},{6,7},{7,6},{8,9},{9,8},{10,11... | collective-permute-start | bytes 2064392 | tf_op jit(solution)/shard_map/ppermute | solution.py:16
  116.4 7.3 %collective-permute-start.10 = (bf16[96,3584]{1,0:T(8,128)(2,1)S(1)}, bf16[96,3584]{1,0:T(8,128)(2,1)S(1)}, u32[]{:S(2)}, u32[]{:S(2)}) collective-permute-start(bf16[96,3584]{1,0:T(8,128)(2,1)S(1)} %collective-permute-done.8.p1), channel_id=1, source_target_pairs={{0,1},{1,0},{2,3},{3,2},{4,5},{5,4},{6,7},{7,6},{8,9},{9,8},{10,11... | collective-permute-start | bytes 2064392 | tf_op jit(solution)/shard_map/ppermute | solution.py:16
  121.7 17.7 %collective-permute-start.23 = (bf16[48,3584]{1,0:T(8,128)(2,1)S(1)}, bf16[48,3584]{1,0:T(8,128)(2,1)S(1)}, u32[]{:S(2)}, u32[]{:S(2)}) collective-permute-start(bf16[48,3584]{1,0:T(8,128)(2,1)S(1)} %add_convert_fusion.11), channel_id=1, source_target_pairs={{0,4},{1,5},{2,6},{3,7},{4,8},{5,9},{6,10},{7,11},{8,12},{9,13},{1... | collective-permute-start | bytes 1032200 | tf_op jit(solution)/shard_map/ppermute | solution.py:16
  123.1 16.4 %collective-permute-start.17 = (bf16[48,3584]{1,0:T(8,128)(2,1)S(1)}, bf16[48,3584]{1,0:T(8,128)(2,1)S(1)}, u32[]{:S(2)}, u32[]{:S(2)}) collective-permute-start(bf16[48,3584]{1,0:T(8,128)(2,1)S(1)} %add_convert_fusion.13), channel_id=1, source_target_pairs={{0,2},{1,3},{2,0},{3,1},{4,6},{5,7},{6,4},{7,5},{8,10},{9,11},{10,... | collective-permute-start | bytes 1032200 | tf_op jit(solution)/shard_map/ppermute | solution.py:16
  139.3 2.2 collective-permute-start.11
  139.6 12.3 %collective-permute-start.24 = (bf16[48,3584]{1,0:T(8,128)(2,1)S(1)}, bf16[48,3584]{1,0:T(8,128)(2,1)S(1)}, u32[]{:S(2)}, u32[]{:S(2)}) collective-permute-start(bf16[48,3584]{1,0:T(8,128)(2,1)S(1)} %add_convert_fusion.10), channel_id=1, source_target_pairs={{0,4},{1,5},{2,6},{3,7},{4,8},{5,9},{6,10},{7,11},{8,12},{9,13},{1... | collective-permute-start | bytes 1032200 | tf_op jit(solution)/shard_map/ppermute | solution.py:16
  141.6 11.0 %collective-permute-start.12 = (bf16[48,3584]{1,0:T(8,128)(2,1)S(1)}, bf16[48,3584]{1,0:T(8,128)(2,1)S(1)}, u32[]{:S(2)}, u32[]{:S(2)}) collective-permute-start(bf16[48,3584]{1,0:T(8,128)(2,1)S(1)} %add_convert_fusion.14), channel_id=1, source_target_pairs={{0,2},{1,3},{2,0},{3,1},{4,6},{5,7},{6,4},{7,5},{8,10},{9,11},{10,... | collective-permute-start | bytes 1032200 | tf_op jit(solution)/shard_map/ppermute | solution.py:16
  143.3 15.9 %collective-permute-start.4 = (bf16[48,3584]{1,0:T(8,128)(2,1)S(1)}, bf16[48,3584]{1,0:T(8,128)(2,1)S(1)}, u32[]{:S(2)}, u32[]{:S(2)}) collective-permute-start(bf16[48,3584]{1,0:T(8,128)(2,1)S(1)} %add_convert_fusion.15), channel_id=1, source_target_pairs={{0,2},{1,3},{2,0},{3,1},{4,6},{5,7},{6,4},{7,5},{8,10},{9,11},{10,... | collective-permute-start | bytes 1032200 | tf_op jit(solution)/shard_map/ppermute | solution.py:16
  152.8 10.8 %collective-permute-start.25 = (bf16[48,3584]{1,0:T(8,128)(2,1)S(1)}, bf16[48,3584]{1,0:T(8,128)(2,1)S(1)}, u32[]{:S(2)}, u32[]{:S(2)}) collective-permute-start(bf16[48,3584]{1,0:T(8,128)(2,1)S(1)} %add_convert_fusion.9), channel_id=1, source_target_pairs={{0,4},{1,5},{2,6},{3,7},{4,8},{5,9},{6,10},{7,11},{8,12},{9,13},{1... | collective-permute-start | bytes 1032200 | tf_op jit(solution)/shard_map/ppermute | solution.py:16
  163.8 9.9 %collective-permute-start.31 = (bf16[48,3584]{1,0:T(8,128)(2,1)S(1)}, bf16[48,3584]{1,0:T(8,128)(2,1)S(1)}, u32[]{:S(2)}, u32[]{:S(2)}) collective-permute-start(bf16[48,3584]{1,0:T(8,128)(2,1)S(1)} %add_convert_fusion.8.p0), channel_id=1, source_target_pairs={{0,4},{1,5},{2,6},{3,7},{4,8},{5,9},{6,10},{7,11},{8,12},{9,13},{1... | collective-permute-start | bytes 1032200 | tf_op jit(solution)/shard_map/ppermute | solution.py:16
  173.7 10.8 %collective-permute-start.44 = (bf16[48,3584]{1,0:T(8,128)(2,1)S(1)}, bf16[48,3584]{1,0:T(8,128)(2,1)S(1)}, u32[]{:S(2)}, u32[]{:S(2)}) collective-permute-start(bf16[48,3584]{1,0:T(8,128)(2,1)S(1)} %collective-permute-done.31.p0), channel_id=1, source_target_pairs={{0,2},{1,3},{2,0},{3,1},{4,6},{5,7},{6,4},{7,5},{8,10},{9,11},{10,... | collective-permute-start | bytes 1032200 | tf_op jit(solution)/shard_map/ppermute | solution.py:16
  175.2 13.0 %collective-permute-start.26 = (bf16[48,3584]{1,0:T(8,128)(2,1)S(1)}, bf16[48,3584]{1,0:T(8,128)(2,1)S(1)}, u32[]{:S(2)}, u32[]{:S(2)}) collective-permute-start(bf16[48,3584]{1,0:T(8,128)(2,1)S(1)} %add_convert_fusion.8.p0), channel_id=1, source_target_pairs={{0,2},{1,3},{2,0},{3,1},{4,6},{5,7},{6,4},{7,5},{8,10},{9,11},{10,... | collective-permute-start | bytes 1032200 | tf_op jit(solution)/shard_map/ppermute | solution.py:16
  175.7 12.5 %collective-permute-start.45 = (bf16[48,3584]{1,0:T(8,128)(2,1)S(1)}, bf16[48,3584]{1,0:T(8,128)(2,1)S(1)}, u32[]{:S(2)}, u32[]{:S(2)}) collective-permute-start(bf16[48,3584]{1,0:T(8,128)(2,1)S(1)} %collective-permute-done.31.p0), channel_id=1, source_target_pairs={{0,1},{1,0},{2,3},{3,2},{4,5},{5,4},{6,7},{7,6},{8,9},{9,8},{10,11... | collective-permute-start | bytes 1032200 | tf_op jit(solution)/shard_map/ppermute | solution.py:16
  184.5 3.7 %collective-permute-start.46 = (bf16[48,3584]{1,0:T(8,128)(2,1)S(1)}, bf16[48,3584]{1,0:T(8,128)(2,1)S(1)}, u32[]{:S(2)}, u32[]{:S(2)}) collective-permute-start(bf16[48,3584]{1,0:T(8,128)(2,1)S(1)} %collective-permute-done.44.p1), channel_id=1, source_target_pairs={{0,1},{1,0},{2,3},{3,2},{4,5},{5,4},{6,7},{7,6},{8,9},{9,8},{10,11... | collective-permute-start | bytes 1032200 | tf_op jit(solution)/shard_map/ppermute | solution.py:16
  184.5 19.9 %collective-permute-start.27 = (bf16[48,3584]{1,0:T(8,128)(2,1)S(1)}, bf16[48,3584]{1,0:T(8,128)(2,1)S(1)}, u32[]{:S(2)}, u32[]{:S(2)}) collective-permute-start(bf16[48,3584]{1,0:T(8,128)(2,1)S(1)} %add_convert_fusion.8.p0), channel_id=1, source_target_pairs={{0,1},{1,0},{2,3},{3,2},{4,5},{5,4},{6,7},{7,6},{8,9},{9,8},{10,11... | collective-permute-start | bytes 1032200 | tf_op jit(solution)/shard_map/ppermute | solution.py:16
  185.0 17.9 %collective-permute-start.32 = (bf16[48,3584]{1,0:T(8,128)(2,1)S(1)}, bf16[48,3584]{1,0:T(8,128)(2,1)S(1)}, u32[]{:S(2)}, u32[]{:S(2)}) collective-permute-start(bf16[48,3584]{1,0:T(8,128)(2,1)S(1)} %collective-permute-done.31.p0), channel_id=1, source_target_pairs={{0,4},{1,5},{2,6},{3,7},{4,8},{5,9},{6,10},{7,11},{8,12},{9,13},{1... | collective-permute-start | bytes 1032200 | tf_op jit(solution)/shard_map/ppermute | solution.py:16
  188.2 16.3 %collective-permute-start.28 = (bf16[48,3584]{1,0:T(8,128)(2,1)S(1)}, bf16[48,3584]{1,0:T(8,128)(2,1)S(1)}, u32[]{:S(2)}, u32[]{:S(2)}) collective-permute-start(bf16[48,3584]{1,0:T(8,128)(2,1)S(1)} %collective-permute-done.26.p1), channel_id=1, source_target_pairs={{0,1},{1,0},{2,3},{3,2},{4,5},{5,4},{6,7},{7,6},{8,9},{9,8},{10,11... | collective-permute-start | bytes 1032200 | tf_op jit(solution)/shard_map/ppermute | solution.py:16
  202.4 17.4 %collective-permute-start.47 = (bf16[96,3584]{1,0:T(8,128)(2,1)S(1)}, bf16[96,3584]{1,0:T(8,128)(2,1)S(1)}, u32[]{:S(2)}, u32[]{:S(2)}) collective-permute-start(bf16[96,3584]{1,0:T(8,128)(2,1)S(1)} %get-tuple-element.49), channel_id=1, source_target_pairs={{0,1},{1,0},{2,3},{3,2},{4,5},{5,4},{6,7},{7,6},{8,9},{9,8},{10,11... | collective-permute-start | bytes 2064392 | tf_op jit(solution)/shard_map/ppermute | solution.py:16
  202.9 16.8 %collective-permute-start.39 = (bf16[48,3584]{1,0:T(8,128)(2,1)S(1)}, bf16[48,3584]{1,0:T(8,128)(2,1)S(1)}, u32[]{:S(2)}, u32[]{:S(2)}) collective-permute-start(bf16[48,3584]{1,0:T(8,128)(2,1)S(1)} %collective-permute-done.32.p0), channel_id=1, source_target_pairs={{0,2},{1,3},{2,0},{3,1},{4,6},{5,7},{6,4},{7,5},{8,10},{9,11},{10,... | collective-permute-start | bytes 1032200 | tf_op jit(solution)/shard_map/ppermute | solution.py:16
  204.4 14.8 %collective-permute-start.33 = (bf16[48,3584]{1,0:T(8,128)(2,1)S(1)}, bf16[48,3584]{1,0:T(8,128)(2,1)S(1)}, u32[]{:S(2)}, u32[]{:S(2)}) collective-permute-start(bf16[48,3584]{1,0:T(8,128)(2,1)S(1)} %collective-permute-done.32.p0), channel_id=1, source_target_pairs={{0,4},{1,5},{2,6},{3,7},{4,8},{5,9},{6,10},{7,11},{8,12},{9,13},{1... | collective-permute-start | bytes 1032200 | tf_op jit(solution)/shard_map/ppermute | solution.py:16
  218.6 38.8 %collective-permute-start.29 = (bf16[96,3584]{1,0:T(8,128)(2,1)S(1)}, bf16[96,3584]{1,0:T(8,128)(2,1)S(1)}, u32[]{:S(2)}, u32[]{:S(2)}) collective-permute-start(bf16[96,3584]{1,0:T(8,128)(2,1)S(1)} %get-tuple-element.37), channel_id=1, source_target_pairs={{0,1},{1,0},{2,3},{3,2},{4,5},{5,4},{6,7},{7,6},{8,9},{9,8},{10,11... | collective-permute-start | bytes 2064392 | tf_op jit(solution)/shard_map/ppermute | solution.py:16
  218.7 2.6 collective-permute-start.40
  219.2 17.5 %collective-permute-start.34 = (bf16[48,3584]{1,0:T(8,128)(2,1)S(1)}, bf16[48,3584]{1,0:T(8,128)(2,1)S(1)}, u32[]{:S(2)}, u32[]{:S(2)}) collective-permute-start(bf16[48,3584]{1,0:T(8,128)(2,1)S(1)} %collective-permute-done.33.p0), channel_id=1, source_target_pairs={{0,2},{1,3},{2,0},{3,1},{4,6},{5,7},{6,4},{7,5},{8,10},{9,11},{10,... | collective-permute-start | bytes 1032200 | tf_op jit(solution)/shard_map/ppermute | solution.py:16
  219.7 20.2 %collective-permute-start.35 = (bf16[48,3584]{1,0:T(8,128)(2,1)S(1)}, bf16[48,3584]{1,0:T(8,128)(2,1)S(1)}, u32[]{:S(2)}, u32[]{:S(2)}) collective-permute-start(bf16[48,3584]{1,0:T(8,128)(2,1)S(1)} %collective-permute-done.33.p0), channel_id=1, source_target_pairs={{0,1},{1,0},{2,3},{3,2},{4,5},{5,4},{6,7},{7,6},{8,9},{9,8},{10,11... | collective-permute-start | bytes 1032200 | tf_op jit(solution)/shard_map/ppermute | solution.py:16
  219.7 2.6 collective-permute-start.41
  221.3 15.7 %collective-permute-start.48 = (bf16[48,3584]{1,0:T(8,128)(2,1)S(1)}, bf16[48,3584]{1,0:T(8,128)(2,1)S(1)}, u32[]{:S(2)}, u32[]{:S(2)}) collective-permute-start(bf16[48,3584]{1,0:T(8,128)(2,1)S(1)} %add_convert_fusion.4), channel_id=1, source_target_pairs={{0,2},{1,3},{2,0},{3,1},{4,6},{5,7},{6,4},{7,5},{8,10},{9,11},{10,... | collective-permute-start | bytes 1032200 | tf_op jit(solution)/shard_map/ppermute | solution.py:16
  236.5 2.2 collective-permute-start.42
  236.7 3.2 %collective-permute-start.36 = (bf16[48,3584]{1,0:T(8,128)(2,1)S(1)}, bf16[48,3584]{1,0:T(8,128)(2,1)S(1)}, u32[]{:S(2)}, u32[]{:S(2)}) collective-permute-start(bf16[48,3584]{1,0:T(8,128)(2,1)S(1)} %collective-permute-done.34.p1), channel_id=1, source_target_pairs={{0,1},{1,0},{2,3},{3,2},{4,5},{5,4},{6,7},{7,6},{8,9},{9,8},{10,11... | collective-permute-start | bytes 1032200 | tf_op jit(solution)/shard_map/ppermute | solution.py:16
  237.2 17.0 %collective-permute-start.49 = (bf16[48,3584]{1,0:T(8,128)(2,1)S(1)}, bf16[48,3584]{1,0:T(8,128)(2,1)S(1)}, u32[]{:S(2)}, u32[]{:S(2)}) collective-permute-start(bf16[48,3584]{1,0:T(8,128)(2,1)S(1)} %add_convert_fusion.3), channel_id=1, source_target_pairs={{0,4},{1,5},{2,6},{3,7},{4,8},{5,9},{6,10},{7,11},{8,12},{9,13},{1... | collective-permute-start | bytes 1032200 | tf_op jit(solution)/shard_map/ppermute | solution.py:16
  238.8 15.4 %collective-permute-start.43 = (bf16[48,3584]{1,0:T(8,128)(2,1)S(1)}, bf16[48,3584]{1,0:T(8,128)(2,1)S(1)}, u32[]{:S(2)}, u32[]{:S(2)}) collective-permute-start(bf16[48,3584]{1,0:T(8,128)(2,1)S(1)} %add_convert_fusion.5), channel_id=1, source_target_pairs={{0,2},{1,3},{2,0},{3,1},{4,6},{5,7},{6,4},{7,5},{8,10},{9,11},{10,... | collective-permute-start | bytes 1032200 | tf_op jit(solution)/shard_map/ppermute | solution.py:16
  254.1 2.2 collective-permute-start.37
  254.3 12.6 %collective-permute-start.50 = (bf16[48,3584]{1,0:T(8,128)(2,1)S(1)}, bf16[48,3584]{1,0:T(8,128)(2,1)S(1)}, u32[]{:S(2)}, u32[]{:S(2)}) collective-permute-start(bf16[48,3584]{1,0:T(8,128)(2,1)S(1)} %add_convert_fusion.2), channel_id=1, source_target_pairs={{0,4},{1,5},{2,6},{3,7},{4,8},{5,9},{6,10},{7,11},{8,12},{9,13},{1... | collective-permute-start | bytes 1032200 | tf_op jit(solution)/shard_map/ppermute | solution.py:16
  256.4 11.0 %collective-permute-start.38 = (bf16[48,3584]{1,0:T(8,128)(2,1)S(1)}, bf16[48,3584]{1,0:T(8,128)(2,1)S(1)}, u32[]{:S(2)}, u32[]{:S(2)}) collective-permute-start(bf16[48,3584]{1,0:T(8,128)(2,1)S(1)} %add_convert_fusion.6), channel_id=1, source_target_pairs={{0,2},{1,3},{2,0},{3,1},{4,6},{5,7},{6,4},{7,5},{8,10},{9,11},{10,... | collective-permute-start | bytes 1032200 | tf_op jit(solution)/shard_map/ppermute | solution.py:16
  257.5 16.4 %collective-permute-start.30 = (bf16[48,3584]{1,0:T(8,128)(2,1)S(1)}, bf16[48,3584]{1,0:T(8,128)(2,1)S(1)}, u32[]{:S(2)}, u32[]{:S(2)}) collective-permute-start(bf16[48,3584]{1,0:T(8,128)(2,1)S(1)} %add_convert_fusion.7), channel_id=1, source_target_pairs={{0,2},{1,3},{2,0},{3,1},{4,6},{5,7},{6,4},{7,5},{8,10},{9,11},{10,... | collective-permute-start | bytes 1032200 | tf_op jit(solution)/shard_map/ppermute | solution.py:16
  267.5 11.3 %collective-permute-start.51 = (bf16[48,3584]{1,0:T(8,128)(2,1)S(1)}, bf16[48,3584]{1,0:T(8,128)(2,1)S(1)}, u32[]{:S(2)}, u32[]{:S(2)}) collective-permute-start(bf16[48,3584]{1,0:T(8,128)(2,1)S(1)} %add_convert_fusion.1), channel_id=1, source_target_pairs={{0,4},{1,5},{2,6},{3,7},{4,8},{5,9},{6,10},{7,11},{8,12},{9,13},{1... | collective-permute-start | bytes 1032200 | tf_op jit(solution)/shard_map/ppermute | solution.py:16
  279.0 13.9 %copy-start.7 = (bf16[48,3584]{1,0:T(8,128)(2,1)}, bf16[48,3584]{1,0:T(8,128)(2,1)S(1)}, u32[]{:S(2)}) copy-start(bf16[48,3584]{1,0:T(8,128)(2,1)S(1)} %add_convert_fusion) | copy-start | bytes 1032196
